TPU v7x, 512 devices: a whole 4x4x16 slice. The times are simulated.
512 devices in a mesh: snap: 16 (over x, y), vert: 32 (over z, core).
Axes of the slice: x: 4, y: 4, z: 16, core: 2. Of those that a mesh axis runs over, the one named last changes fastest.
Arguments:
- features: bfloat16 [16, 16384, 256], P('snap', 'vert'), may hold values from -6 to 6
- tile_src: int32 [16, 1024], P('snap', 'vert'), may hold values from 0 to 127, as said below
- tile_dst: int32 [16, 1024], P('snap', 'vert'), may hold values from 0 to 127, as said below
- tile_count: int32 [16, 32], P('snap', 'vert'), may hold values from 4 to 32, as said below
- tile_vals: bfloat16 [16, 1024, 128, 128], P('snap', 'vert'), may hold values from -0.25 to 0.25
- norm_gain: float32 [256], replicated, may hold values from 0.25 to 1.75
- mix_weight: bfloat16 [256, 512], replicated, may hold values from -0.375 to 0.375
- decay_rate: float32 [16, 256], replicated, may hold values from 0 to 9, as said below
- mlp_gain: float32 [256], replicated, may hold values from 0.25 to 1.75
- up_weight: bfloat16 [256, 1024], replicated, may hold values from -0.375 to 0.375
- down_weight: bfloat16 [1024, 256], replicated, may hold values from -0.1875 to 0.1875
- link_weight: bfloat16 [256, 256], replicated, may hold values from -0.375 to 0.375
- pair_left: int32 [16, 1024], P('snap', 'vert'), may hold values from 0 to 127, as said below
- pair_right: int32 [16, 1024], P('snap', 'vert'), may hold values from 0 to 127, as said below
Outputs:
- embeddings: bfloat16 [16, 16384, 256], P('snap', 'vert')
- scores: bfloat16 [16, 1024, 128, 128], P('snap', 'vert')
Inputs may be any that keep to these rules, and one draw needn't show every extreme that they name: `tile_src`: a slot of vertex part p names a source block from p * 4 - 4 to p * 4 + 2 * 4 - 1. `tile_dst`: a slot of vertex part p names a destination block of that part, p * 4 to p * 4 + 3. `tile_count`: in every snapshot some vertex part has all 32 slots live. `decay_rate`: decay rates are positive. `pair_left`: a pair of vertex part p has its first block in that part, p * 4 to p * 4 + 3. `pair_right`: a pair of vertex part p has its second block from p * 4 - 4 to p * 4 + 2 * 4 - 1.
All inputs are finite; a program needn't handle non-finite values.
Results may differ from a plain program's by a relative error of at most 0.0091.
Values may be sent and summed in bfloat16 or wider, within the bound.
No kernel may reach another device: no remote copies, remote signals or barrier semaphores. Data moves between devices by JAX's collectives and lax.ppermute only.
A program may use at most 64 MiB of HBM per device.

v0:
```python
import jax
import jax.numpy as jnp
from jax import lax
from jax.sharding import PartitionSpec as P

epsilon = 1e-06


def with_halo(cells, sides, width):
    for axis, dim in sides:
        count = lax.axis_size(axis)
        ends = count - 1
        head = lax.slice_in_dim(cells, 0, width, axis=dim)
        tail = lax.slice_in_dim(cells, cells.shape[dim] - width, cells.shape[dim], axis=dim)
        cells = jnp.concatenate(
            [
                lax.ppermute(tail, axis, [(i, (i + 1) % count) for i in range(ends)]),
                cells,
                lax.ppermute(head, axis, [((i + 1) % count, i) for i in range(ends)]),
            ],
            axis=dim,
        )
    return cells


def root_norm(values, gain_vector):
    return (
        values
        * lax.rsqrt(jnp.mean(values * values, axis=-1, keepdims=True) + epsilon)
        * gain_vector
    )


def pick_blocks(blocks, indices):
    return jax.vmap(lambda source_table, chosen: jnp.take(source_table, chosen, axis=0))(
        blocks, indices
    )


def tile_terms(blocks, src_index, dst_index, tile_part, alive_slots, per_part):
    picked = pick_blocks(blocks, src_index)
    product = jnp.einsum("sgij,sgjf->sgif", tile_part, picked, preferred_element_type=jnp.float32)
    targets = jnp.arange(per_part, dtype=jnp.int32)[None, None, :]
    selector = ((dst_index[:, :, None] == targets) & alive_slots[:, :, None]).astype(jnp.float32)
    return jnp.einsum("sgb,sgif->sbif", selector, product, precision=lax.Precision.HIGHEST)


def gate_drive(normed, step_rates, mix_weight):
    projected = jnp.einsum("tnf,fg->tng", normed, mix_weight, preferred_element_type=jnp.float32)
    feature_width = normed.shape[-1]
    decays = jnp.exp(-step_rates[:, None, :] * jax.nn.sigmoid(projected[..., :feature_width]))
    return (decays, (1.0 - decays) * projected[..., feature_width:])


def advance(previous, inputs):
    updated = inputs[0] * previous + inputs[1]
    return (updated, updated)


def run_states(decays, drives, start_state):
    final_state, states = lax.scan(advance, start_state, (decays, drives))
    return states


def feed_forward(states, mlp_gain, up_weight, down_weight):
    state_normed = root_norm(states, mlp_gain).astype(jnp.bfloat16)
    hidden = jax.nn.silu(
        jnp.einsum("tnf,fh->tnh", state_normed, up_weight, preferred_element_type=jnp.float32)
    ).astype(jnp.bfloat16)
    return (
        states + jnp.einsum("tnh,hf->tnf", hidden, down_weight, preferred_element_type=jnp.float32)
    ).astype(jnp.bfloat16)


def body(
    features,
    tile_src,
    tile_dst,
    tile_count,
    tile_vals,
    norm_gain,
    mix_weight,
    decay_rate,
    mlp_gain,
    up_weight,
    down_weight,
    link_weight,
    pair_left,
    pair_right,
):
    snaps_here, vertices_here, feature_width = features.shape
    tile_rows = tile_vals.shape[-1]
    slot_count = tile_vals.shape[1]
    per_part = vertices_here // tile_rows
    part_index = lax.axis_index("vert")
    first_block = (part_index - 1) * per_part
    own_first = part_index * per_part
    extended = with_halo(features, (("vert", 1),), vertices_here)
    blocks = extended.reshape(snaps_here, 3 * per_part, tile_rows, feature_width)
    local_src = tile_src - first_block
    local_dst = tile_dst - own_first
    slot_ids = jnp.arange(slot_count, dtype=jnp.int32)[None, :]
    aggregate = tile_terms(blocks, local_src, local_dst, tile_vals, slot_ids < tile_count, per_part)
    combined = aggregate.reshape(snaps_here, vertices_here, feature_width) + features.astype(
        jnp.float32
    )
    normed = root_norm(combined, norm_gain).astype(jnp.bfloat16)
    by_vertex = lax.all_to_all(normed, "snap", split_axis=1, concat_axis=0, tiled=True)
    decays, drives = gate_drive(by_vertex, decay_rate, mix_weight)
    states = run_states(decays, drives, jnp.zeros(decays.shape[1:], jnp.float32))
    vertex_out = feed_forward(states, mlp_gain, up_weight, down_weight)
    embeddings = lax.all_to_all(vertex_out, "snap", split_axis=0, concat_axis=1, tiled=True)
    extended_out = with_halo(embeddings, (("vert", 1),), vertices_here)
    left_side = jnp.einsum(
        "svf,fg->svg", embeddings, link_weight, preferred_element_type=jnp.float32
    ).astype(jnp.bfloat16)
    left_blocks = pick_blocks(
        left_side.reshape(snaps_here, per_part, tile_rows, feature_width), pair_left - own_first
    )
    right_blocks = pick_blocks(
        extended_out.reshape(snaps_here, 3 * per_part, tile_rows, feature_width),
        pair_right - first_block,
    )
    scores = jnp.einsum(
        "spif,spjf->spij", left_blocks, right_blocks, preferred_element_type=jnp.float32
    ) * feature_width ** (-0.5)
    return (embeddings, scores.astype(jnp.bfloat16))


def solution(mesh):
    return jax.shard_map(
        body,
        mesh=mesh,
        in_specs=(
            P("snap", "vert", None),
            P("snap", "vert"),
            P("snap", "vert"),
            P("snap", "vert"),
            P("snap", "vert", None, None),
            P(),
            P(),
            P(),
            P(),
            P(),
            P(),
            P(),
            P("snap", "vert"),
            P("snap", "vert"),
        ),
        out_specs=(P("snap", "vert", None), P("snap", "vert", None, None)),
        check_vma=False,
    )
```

profile of v0, /device:TPU:97, one launch (start us, length us, event | category | flops | bytes accessed | tf_op | source)
XLA Modules:
  0.0 86.9 jit_solution(15219343378757450271)
XLA Ops:
  0.6 0.0 copy-start
  0.6 5.5 %collective-permute-start = (bf16[1,512,256]{2,1,0:T(8,128)(2,1)}, bf16[1,512,256]{2,1,0:T(8,128)(2,1)S(1)}, u32[]{:S(2)}, u32[]{:S(2)}) collective-permute-start(bf16[1,512,256]{2,1,0:T(8,128)(2,1)} %param.18), channel_id=1, source_target_pairs={{0,1},{1,2},{2,3},{3,4},{4,5},{5,6},{6,7},{7,8},{8,9},{9,10},{10,1... | collective-permute-start | bytes 786440 | tf_op jit(solution)/shard_map/ppermute | solution.py:17
  6.1 1.9 %collective-permute-start.1 = (bf16[1,512,256]{2,1,0:T(8,128)(2,1)}, bf16[1,512,256]{2,1,0:T(8,128)(2,1)S(1)}, u32[]{:S(2)}, u32[]{:S(2)}) collective-permute-start(bf16[1,512,256]{2,1,0:T(8,128)(2,1)} %param.18), channel_id=1, source_target_pairs={{1,0},{2,1},{3,2},{4,3},{5,4},{6,5},{7,6},{8,7},{9,8},{10,9},{11,1... | collective-permute-start | bytes 786440 | tf_op jit(solution)/shard_map/ppermute | solution.py:19
  8.0 0.7 and_bitcast_fusion.1
  9.4 0.7 subtract_bitcast_fusion
  10.0 0.7 neg.11
  10.8 0.0 collective-permute-done
  10.8 4.4 %collective-permute-done.1 = bf16[1,512,256]{2,1,0:T(8,128)(2,1)S(1)} collective-permute-done((bf16[1,512,256]{2,1,0:T(8,128)(2,1)}, bf16[1,512,256]{2,1,0:T(8,128)(2,1)S(1)}, u32[]{:S(2)}, u32[]{:S(2)}) %collective-permute-start.1) | collective-permute-done | bytes 262176 | tf_op jit(solution)/shard_map/ppermute | solution.py:19
  15.2 1.0 %pad_maximum_fusion = bf16[1,1536,256]{2,1,0:T(8,128)(2,1)S(1)} fusion(bf16[1,512,256]{2,1,0:T(8,128)(2,1)S(1)} %collective-permute-done.1, bf16[1,512,256]{2,1,0:T(8,128)(2,1)} %param.18, bf16[1,512,256]{2,1,0:T(8,128)(2,1)S(1)} %collective-permute-done), kind=kLoop, calls=%fused_computation.27 | loop fusion | flops 2359296 | bytes 1572864 | tf_op jit(solution)/shard_map/concatenate | solution.py:15
  16.2 2.0 %gather_fusion.1 = bf16[32,128,256]{2,1,0:T(8,128)(2,1)} fusion(bf16[1,12,128,256]{3,2,1,0:T(8,128)(2,1)S(1)} %bitcast.104, s32[32]{0:T(128)S(1)} %or_bitcast_fusion.1), kind=kCustom, calls=%fused_computation.clone | custom fusion | bytes 4194560 | tf_op jit(solution)/shard_map/vmap(jit(_take))/gather | solution.py:35
  18.2 0.0 copy-done
  18.2 4.4 %convolution_bitcast_fusion = f32[32,128,256]{1,2,0:T(8,128)} fusion(bf16[32,128,256]{2,1,0:T(8,128)(2,1)} %gather_fusion.1, pred[32]{0:T(512)(128)(4,1)S(1)} %get-tuple-element.67, bf16[1,32,128,128]{3,2,1,0:T(8,128)(2,1)S(1)} %copy-done), kind=kOutput, calls=%fused_computation.6 | convolution fusion | flops 269484032 | bytes 7340064 | tf_op jit(solution)/shard_map/sgij,sgjf->sgif/dot_general | solution.py:42
  22.6 5.5 %copy.21 = f32[32,128,256]{2,0,1:T(8,128)} copy(f32[32,128,256]{1,2,0:T(8,128)} %convolution_bitcast_fusion) | data formatting | bytes 8388608 | tf_op jit(solution)/shard_map/sgij,sgjf->sgif/dot_general | solution.py:42
  28.1 3.7 %fusion.38 = f32[4,128,256]{2,0,1:T(4,128)S(1)} fusion(f32[32,128,256]{2,0,1:T(8,128)} %copy.21, s32[32]{0:T(128)S(1)} %subtract_bitcast_fusion, pred[32]{0:T(512)(128)(4,1)S(1)} %iota_compare_fusion.1), kind=kOutput, calls=%fused_computation.55 | convolution fusion | flops 50331904 | bytes 4718752 | tf_op jit(solution)/shard_map/sgb,sgif->sbif/dot_general | solution.py:45
  31.8 0.1 copy.22
  31.9 0.0 copy-done.1
  31.9 0.0 copy-start.5
  31.9 0.0 copy-start.6
  31.9 0.2 multiply_reduce_fusion.1
  32.1 0.1 multiply_convert_fusion.5
  32.2 0.0 copy-start.2
  32.3 0.4 copy.27
  32.7 0.5 broadcast.170
  33.2 2.2 %reduce.1 = bf16[512,256]{1,0:T(8,128)(2,1)S(1)} reduce(bf16[512,1,256]{2,1,0:T(2,128)(2,1)S(1)} %bitcast.114, bf16[]{:T(256)} %broadcast.170), dimensions={1}, to_apply=%bitcast.97.reduce_sub_computation | reduce | bytes 524290
  35.4 0.8 reshape.205
  36.2 6.8 %all-to-all-start = ((bf16[16,2,4096]{2,1,0:T(2,128)(2,1)}), bf16[16,2,4096]{2,1,0:T(2,128)(2,1)S(1)}, u32[]{:S(2)}, u32[]{:S(2)}) async-start(bf16[16,2,4096]{2,1,0:T(2,128)(2,1)} %reshape.205), calls=%async_computation | async-start | bytes 524288 | tf_op jit(solution)/shard_map/all_to_all | solution.py:108
  43.0 7.3 %all-to-all-done = bf16[16,2,4096]{2,1,0:T(2,128)(2,1)S(1)} async-done(((bf16[16,2,4096]{2,1,0:T(2,128)(2,1)}), bf16[16,2,4096]{2,1,0:T(2,128)(2,1)S(1)}, u32[]{:S(2)}, u32[]{:S(2)}) %all-to-all-start) | async-done | bytes 262176 | tf_op jit(solution)/shard_map/all_to_all | solution.py:108
  50.3 0.3 reshape.206
  50.6 0.0 copy-done.2
  50.6 0.3 fusion.30
  50.9 0.0 copy-start.7
  50.9 0.2 slice_multiply_fusion
  51.1 0.6 while.13
  51.8 0.1 multiply_reduce_fusion
  52.0 0.0 copy-start.3
  52.0 2.8 %fusion.16 = bf16[16,32,256]{2,1,0:T(8,128)(2,1)} fusion(f32[16,32,256]{2,1,0:T(8,128)S(1)} %get-tuple-element.30, bf16[1024,256]{1,0:T(8,128)(2,1)} %param.28, bf16[256,1024]{1,0:T(8,128)(2,1)} %param.27, f32[256]{0:T(256)S(1)} %copy-done.7, f32[16,32]{1,0:T(8,128)S(1)} %add_rsqrt_fusion), kind=kOutput, calls=%fused_computation.20 | convolution fusion | flops 540147712 | bytes 1838080 | tf_op jit(solution)/shard_map/tnh,hf->tnf/dot_general | solution.py:71
  54.8 3.5 %all-to-all-start.1 = ((bf16[16,32,256]{2,1,0:T(8,128)(2,1)}), bf16[16,32,256]{2,1,0:T(8,128)(2,1)S(1)}, u32[]{:S(2)}, u32[]{:S(2)}) async-start(bf16[16,32,256]{2,1,0:T(8,128)(2,1)} %fusion.16), calls=%async_computation.1 | async-start | bytes 524288 | tf_op jit(solution)/shard_map/all_to_all | solution.py:112
  58.4 7.3 %all-to-all-done.1 = bf16[16,32,256]{2,1,0:T(8,128)(2,1)S(1)} async-done(((bf16[16,32,256]{2,1,0:T(8,128)(2,1)}), bf16[16,32,256]{2,1,0:T(8,128)(2,1)S(1)}, u32[]{:S(2)}, u32[]{:S(2)}) %all-to-all-start.1) | async-done | bytes 262176 | tf_op jit(solution)/shard_map/all_to_all | solution.py:112
  65.6 5.6 %collective-permute-start.2 = (bf16[1,512,256]{2,1,0:T(8,128)(2,1)S(1)}, bf16[1,512,256]{2,1,0:T(8,128)(2,1)S(1)}, u32[]{:S(2)}, u32[]{:S(2)}) collective-permute-start(bf16[1,512,256]{2,1,0:T(8,128)(2,1)S(1)} %bitcast.108), channel_id=1, source_target_pairs={{0,1},{1,2},{2,3},{3,4},{4,5},{5,6},{6,7},{7,8},{8,9},{9,10},{10,1... | collective-permute-start | bytes 786440 | tf_op jit(solution)/shard_map/ppermute | solution.py:17
  71.3 1.9 %collective-permute-start.3 = (bf16[1,512,256]{2,1,0:T(8,128)(2,1)S(1)}, bf16[1,512,256]{2,1,0:T(8,128)(2,1)S(1)}, u32[]{:S(2)}, u32[]{:S(2)}) collective-permute-start(bf16[1,512,256]{2,1,0:T(8,128)(2,1)S(1)} %bitcast.109), channel_id=1, source_target_pairs={{1,0},{2,1},{3,2},{4,3},{5,4},{6,5},{7,6},{8,7},{9,8},{10,9},{11,1... | collective-permute-start | bytes 786440 | tf_op jit(solution)/shard_map/ppermute | solution.py:19
  73.2 0.2 convolution_convert_fusion
  73.5 2.0 %gather_fusion = bf16[32,128,256]{2,1,0:T(8,128)(2,1)} fusion(bf16[1,4,128,256]{3,2,1,0:T(8,128)(2,1)S(1)} %bitcast.103, s32[32]{0:T(128)S(1)} %or_bitcast_fusion.2), kind=kCustom, calls=%fused_computation.2 | custom fusion | bytes 4194560 | tf_op jit(solution)/shard_map/vmap(jit(_take))/gather | solution.py:35
  75.5 0.0 collective-permute-done.2
  75.5 4.7 %collective-permute-done.3 = bf16[1,512,256]{2,1,0:T(8,128)(2,1)S(1)} collective-permute-done((bf16[1,512,256]{2,1,0:T(8,128)(2,1)S(1)}, bf16[1,512,256]{2,1,0:T(8,128)(2,1)S(1)}, u32[]{:S(2)}, u32[]{:S(2)}) %collective-permute-start.3) | collective-permute-done | bytes 262176 | tf_op jit(solution)/shard_map/ppermute | solution.py:19
  80.2 0.1 pad_maximum_fusion.1
  80.2 2.0 %gather_fusion.2 = bf16[32,128,256]{2,1,0:T(8,128)(2,1)} fusion(bf16[1,12,128,256]{3,2,1,0:T(8,128)(2,1)S(1)} %bitcast.105, s32[32]{0:T(128)S(1)} %or_bitcast_fusion), kind=kCustom, calls=%fused_computation.1.clone | custom fusion | bytes 4194560 | tf_op jit(solution)/shard_map/vmap(jit(_take))/gather | solution.py:35
  82.2 4.0 %fusion.11 = bf16[1,32,128,128]{3,2,1,0:T(8,128)(2,1)} fusion(bf16[32,128,256]{2,1,0:T(8,128)(2,1)} %gather_fusion.2, pred[32]{0:T(512)(128)(4,1)S(1)} %get-tuple-element.63, bf16[32,128,256]{2,1,0:T(8,128)(2,1)} %gather_fusion, pred[32]{0:T(512)(128)(4,1)S(1)} %get-tuple-element.69), kind=kOutput, calls=%fused_computation.18 | convolution fusion | flops 271581184 | bytes 5242944 | tf_op jit(solution)/shard_map/spif,spjf->spij/dot_general | solution.py:124
  86.2 0.7 copy.40
  (36 shorter events, 0.4 us)
Async XLA Ops:
  0.6 17.6 %copy-start = (bf16[1,32,128,128]{3,2,1,0:T(8,128)(2,1)S(1)}, bf16[1,32,128,128]{3,2,1,0:T(8,128)(2,1)}, u32[]{:S(2)}) copy-start(bf16[1,32,128,128]{3,2,1,0:T(8,128)(2,1)} %param.22) | copy-start | bytes 3145732
  0.6 10.1 %collective-permute-start = (bf16[1,512,256]{2,1,0:T(8,128)(2,1)}, bf16[1,512,256]{2,1,0:T(8,128)(2,1)S(1)}, u32[]{:S(2)}, u32[]{:S(2)}) collective-permute-start(bf16[1,512,256]{2,1,0:T(8,128)(2,1)} %param.18), channel_id=1, source_target_pairs={{0,1},{1,2},{2,3},{3,4},{4,5},{5,6},{6,7},{7,8},{8,9},{9,10},{10,1... | collective-permute-start | bytes 786440 | tf_op jit(solution)/shard_map/ppermute | solution.py:17
  6.1 9.1 %collective-permute-start.1 = (bf16[1,512,256]{2,1,0:T(8,128)(2,1)}, bf16[1,512,256]{2,1,0:T(8,128)(2,1)S(1)}, u32[]{:S(2)}, u32[]{:S(2)}) collective-permute-start(bf16[1,512,256]{2,1,0:T(8,128)(2,1)} %param.18), channel_id=1, source_target_pairs={{1,0},{2,1},{3,2},{4,3},{5,4},{6,5},{7,6},{8,7},{9,8},{10,9},{11,1... | collective-permute-start | bytes 786440 | tf_op jit(solution)/shard_map/ppermute | solution.py:19
  28.1 3.8 %copy-start.1 = (bf16[1,512,256]{2,1,0:T(8,128)(2,1)S(1)}, bf16[1,512,256]{2,1,0:T(8,128)(2,1)}, u32[]{:S(2)}) copy-start(bf16[1,512,256]{2,1,0:T(8,128)(2,1)} %param.18) | copy-start | bytes 786436
  28.1 4.0 %copy-start.4 = (f32[256]{0:T(256)S(1)}, f32[256]{0:T(256)}, u32[]{:S(2)}) copy-start(f32[256]{0:T(256)} %param.23) | copy-start | bytes 3076
  31.9 11.1 %copy-start.5 = (s32[1,32]{1,0:T(1,128)S(1)}, s32[1,32]{1,0:T(1,128)}, u32[]{:S(2)}) copy-start(s32[1,32]{1,0:T(1,128)} %param.31) | copy-start | bytes 388
  31.9 11.1 %copy-start.6 = (s32[1,32]{1,0:T(1,128)S(1)}, s32[1,32]{1,0:T(1,128)}, u32[]{:S(2)}) copy-start(s32[1,32]{1,0:T(1,128)} %param.30) | copy-start | bytes 388
  32.2 18.3 %copy-start.2 = (bf16[256,512]{1,0:T(8,128)(2,1)S(1)}, bf16[256,512]{1,0:T(8,128)(2,1)}, u32[]{:S(2)}) copy-start(bf16[256,512]{1,0:T(8,128)(2,1)} %param.24) | copy-start | bytes 786436
  36.2 14.1 %all-to-all-start = ((bf16[16,2,4096]{2,1,0:T(2,128)(2,1)}), bf16[16,2,4096]{2,1,0:T(2,128)(2,1)S(1)}, u32[]{:S(2)}, u32[]{:S(2)}) async-start(bf16[16,2,4096]{2,1,0:T(2,128)(2,1)} %reshape.205), calls=%async_computation | async-start | bytes 524288 | tf_op jit(solution)/shard_map/all_to_all | solution.py:108
  50.9 1.1 %copy-start.7 = (f32[256]{0:T(256)S(1)}, f32[256]{0:T(256)}, u32[]{:S(2)}) copy-start(f32[256]{0:T(256)} %param.26) | copy-start | bytes 3076
  52.0 21.3 %copy-start.3 = (bf16[256,256]{1,0:T(8,128)(2,1)S(1)}, bf16[256,256]{1,0:T(8,128)(2,1)}, u32[]{:S(2)}) copy-start(bf16[256,256]{1,0:T(8,128)(2,1)} %param.29) | copy-start | bytes 393220
  54.8 10.8 %all-to-all-start.1 = ((bf16[16,32,256]{2,1,0:T(8,128)(2,1)}), bf16[16,32,256]{2,1,0:T(8,128)(2,1)S(1)}, u32[]{:S(2)}, u32[]{:S(2)}) async-start(bf16[16,32,256]{2,1,0:T(8,128)(2,1)} %fusion.16), calls=%async_computation.1 | async-start | bytes 524288 | tf_op jit(solution)/shard_map/all_to_all | solution.py:112
  65.6 9.8 %collective-permute-start.2 = (bf16[1,512,256]{2,1,0:T(8,128)(2,1)S(1)}, bf16[1,512,256]{2,1,0:T(8,128)(2,1)S(1)}, u32[]{:S(2)}, u32[]{:S(2)}) collective-permute-start(bf16[1,512,256]{2,1,0:T(8,128)(2,1)S(1)} %bitcast.108), channel_id=1, source_target_pairs={{0,1},{1,2},{2,3},{3,4},{4,5},{5,6},{6,7},{7,8},{8,9},{9,10},{10,1... | collective-permute-start | bytes 786440 | tf_op jit(solution)/shard_map/ppermute | solution.py:17
  71.3 8.9 %collective-permute-start.3 = (bf16[1,512,256]{2,1,0:T(8,128)(2,1)S(1)}, bf16[1,512,256]{2,1,0:T(8,128)(2,1)S(1)}, u32[]{:S(2)}, u32[]{:S(2)}) collective-permute-start(bf16[1,512,256]{2,1,0:T(8,128)(2,1)S(1)} %bitcast.109), channel_id=1, source_target_pairs={{1,0},{2,1},{3,2},{4,3},{5,4},{6,5},{7,6},{8,7},{9,8},{10,9},{11,1... | collective-permute-start | bytes 786440 | tf_op jit(solution)/shard_map/ppermute | solution.py:19
where the time goes:
time: 87.6 us; the launch traced here: 86.9 us
  starting transfers between devices  25.2 us (29%)
  waiting for transfers between devices  23.7 us (27%)
  matrix products  15.4 us (18%)
  local copies, waits for them, and re-layouts  14.4 us (16%)
  other arithmetic  6.3 us (7%)
  between operations  1.6 us (2%)
    ppermute x2, starting transfers between devices, with_halo(): lax.ppermute(tail, axis, [(i, (i + 1) % count) for i in range(ends)])  11.1 us
    ppermute x2, waiting for transfers between devices, with_halo(): lax.ppermute(head, axis, [((i + 1) % count, i) for i in range(ends)])  9.16 us
    all_to_all x1, waiting for transfers between devices, body(): lax.all_to_all(vertex_out, 'snap', split_axis=0, concat_axis=1, tiled=True)  7.28 us
    all_to_all x1, waiting for transfers between devices, body(): lax.all_to_all(normed, 'snap', split_axis=1, concat_axis=0, tiled=True)  7.26 us
    all_to_all x1, starting transfers between devices, body(): lax.all_to_all(normed, 'snap', split_axis=1, concat_axis=0, tiled=True)  6.75 us
    gather x6, local copies, waits for them, and re-layouts, pick_blocks(): jnp.take(source_table, chosen, axis=0)  6.03 us
    dot_general x1, local copies, waits for them, and re-layouts, tile_terms(): jnp.einsum('sgij,sgjf->sgif', tile_part, picked, preferred_element_type=j...  5.47 us
    dot_general x1, matrix products, tile_terms(): jnp.einsum('sgij,sgjf->sgif', tile_part, picked, preferred_element_type=j...  4.37 us
  transfers between devices with their start and end apart: 6, of which 4 were waited for; matrix products, arithmetic and copies ran while one was open for 5% of the time, Pallas kernels for 0%

commit v1 on v0

--- a/solution.py
+++ b/solution.py
@@ -4,6 +4,28 @@
 from jax.sharding import PartitionSpec as P
 
 epsilon = 1e-06
+
+
+def split_up(array, dim, length):
+    before, after = (array.shape[:dim], array.shape[dim + 1 :])
+    return jnp.moveaxis(array.reshape(*before, length, -1, *after), dim, 0)
+
+
+def laid_out(pieces, dim):
+    pieces = jnp.moveaxis(pieces, 0, dim)
+    shape = pieces.shape
+    return pieces.reshape(*shape[:dim], shape[dim] * shape[dim + 1], *shape[dim + 2 :])
+
+
+def exchange_in_pairs(shard, axis, split_dim, concat_dim):
+    size, mine = (lax.axis_size(axis), lax.axis_index(axis))
+    pieces = split_up(shard, split_dim, size)
+    finished = [pieces[mine]]
+    for step in range(1, size):
+        sent = pieces[mine ^ step]
+        finished.append(lax.ppermute(sent, axis, [(i, i ^ step) for i in range(size)]))
+    pieces = jnp.stack(finished)[mine ^ jnp.arange(size)]
+    return laid_out(pieces, concat_dim)
 
 
 def with_halo(cells, sides, width):
@@ -105,7 +127,7 @@
         jnp.float32
     )
     normed = root_norm(combined, norm_gain).astype(jnp.bfloat16)
-    by_vertex = lax.all_to_all(normed, "snap", split_axis=1, concat_axis=0, tiled=True)
+    by_vertex = exchange_in_pairs(normed, "snap", 1, 0)
     decays, drives = gate_drive(by_vertex, decay_rate, mix_weight)
     states = run_states(decays, drives, jnp.zeros(decays.shape[1:], jnp.float32))
     vertex_out = feed_forward(states, mlp_gain, up_weight, down_weight)

time: 87.6 us -> 135 us (1.54)
  starting transfers between devices: 25.2 us -> 76.7 us
  other arithmetic: 6.3 us -> 4.06 us
  waiting for transfers between devices: 23.7 us -> 22.3 us
    ppermute x0 -> x15, starting transfers between devices: none -> 55.9 us  [exchange_in_pairs(): lax.ppermute(sent, axis, [(i, i ^ step) for i in range(size)])]
    all_to_all x1 -> x0, waiting for transfers between devices: 7.26 us -> none  [body(): lax.all_to_all(normed, 'snap', split_axis=1, concat_axis=0, tiled=True)]
    all_to_all x1 -> x0, starting transfers between devices: 6.75 us -> none  [body(): lax.all_to_all(normed, 'snap', split_axis=1, concat_axis=0, tiled=True)]
    ppermute x0 -> x15, waiting for transfers between devices: none -> 5.81 us  [exchange_in_pairs(): lax.ppermute(sent, axis, [(i, i ^ step) for i in range(size)])]
    ppermute x2, starting transfers between devices: 11.1 us -> 13.5 us  [with_halo(): lax.ppermute(tail, axis, [(i, (i + 1) % count) for i in range(ends)])]
    unnamed x2 -> x1, other arithmetic: 2.21 us -> 0.01 us
    unnamed x21 -> x31, local copies, waits for them, and re-layouts: 2.34 us -> 0.8 us
  transfers between devices with their start and end apart: 6 -> 20, of which waited for: 4 -> 4; matrix products, arithmetic and copies ran while one was open for 5% -> 3% of each run, Pallas kernels for 0% -> 0%
where the time goes in v1:
time: 135 us; the launch traced here: 134 us
  starting transfers between devices  76.7 us (57%)
  waiting for transfers between devices  22.3 us (17%)
  matrix products  15.2 us (11%)
  local copies, waits for them, and re-layouts  13.1 us (10%)
  other arithmetic  4.06 us (3%)
  between operations  1.93 us (1%)
    ppermute x15, starting transfers between devices, exchange_in_pairs(): lax.ppermute(sent, axis, [(i, i ^ step) for i in range(size)])  55.9 us
    ppermute x2, starting transfers between devices, with_halo(): lax.ppermute(tail, axis, [(i, (i + 1) % count) for i in range(ends)])  13.5 us
    ppermute x2, waiting for transfers between devices, with_halo(): lax.ppermute(head, axis, [((i + 1) % count, i) for i in range(ends)])  9.19 us
    all_to_all x1, waiting for transfers between devices, body(): lax.all_to_all(vertex_out, 'snap', split_axis=0, concat_axis=1, tiled=True)  7.32 us
    gather x6, local copies, waits for them, and re-layouts, pick_blocks(): jnp.take(source_table, chosen, axis=0)  6.07 us
    ppermute x15, waiting for transfers between devices, exchange_in_pairs(): lax.ppermute(sent, axis, [(i, i ^ step) for i in range(size)])  5.81 us
    dot_general x1, local copies, waits for them, and re-layouts, tile_terms(): jnp.einsum('sgij,sgjf->sgif', tile_part, picked, preferred_element_type=j...  5.48 us
    dot_general x1, matrix products, tile_terms(): jnp.einsum('sgij,sgjf->sgif', tile_part, picked, preferred_element_type=j...  4.38 us
  transfers between devices with their start and end apart: 20, of which 4 were waited for; matrix products, arithmetic and copies ran while one was open for 3% of the time, Pallas kernels for 0%

profile of v1, /device:TPU:97, one launch (start us, length us, event | category | flops | bytes accessed | tf_op | source)
XLA Modules:
  0.0 133.8 jit_solution(10780688388732971505)
XLA Ops:
  0.6 5.5 %collective-permute-start = (bf16[1,512,256]{2,1,0:T(8,128)(2,1)}, bf16[1,512,256]{2,1,0:T(8,128)(2,1)S(1)}, u32[]{:S(2)}, u32[]{:S(2)}) collective-permute-start(bf16[1,512,256]{2,1,0:T(8,128)(2,1)} %param.18), channel_id=1, source_target_pairs={{0,1},{1,2},{2,3},{3,4},{4,5},{5,6},{6,7},{7,8},{8,9},{9,10},{10,1... | collective-permute-start | bytes 786440 | tf_op jit(solution)/shard_map/ppermute | solution.py:39
  6.1 1.9 %collective-permute-start.1 = (bf16[1,512,256]{2,1,0:T(8,128)(2,1)}, bf16[1,512,256]{2,1,0:T(8,128)(2,1)S(1)}, u32[]{:S(2)}, u32[]{:S(2)}) collective-permute-start(bf16[1,512,256]{2,1,0:T(8,128)(2,1)} %param.18), channel_id=1, source_target_pairs={{1,0},{2,1},{3,2},{4,3},{5,4},{6,5},{7,6},{8,7},{9,8},{10,9},{11,1... | collective-permute-start | bytes 786440 | tf_op jit(solution)/shard_map/ppermute | solution.py:41
  8.0 0.7 and_bitcast_fusion.1
  9.4 0.7 subtract_bitcast_fusion
  10.1 0.7 and_bitcast_fusion
  10.8 4.5 %collective-permute-done.1 = bf16[1,512,256]{2,1,0:T(8,128)(2,1)S(1)} collective-permute-done((bf16[1,512,256]{2,1,0:T(8,128)(2,1)}, bf16[1,512,256]{2,1,0:T(8,128)(2,1)S(1)}, u32[]{:S(2)}, u32[]{:S(2)}) %collective-permute-start.1) | collective-permute-done | bytes 262176 | tf_op jit(solution)/shard_map/ppermute | solution.py:41
  15.2 1.0 pad_maximum_fusion
  16.2 2.0 %gather_fusion.2 = bf16[32,128,256]{2,1,0:T(8,128)(2,1)} fusion(bf16[1,12,128,256]{3,2,1,0:T(8,128)(2,1)S(1)} %bitcast.163, s32[32]{0:T(128)S(1)} %or_bitcast_fusion.1), kind=kCustom, calls=%fused_computation.clone | custom fusion | bytes 4194560 | tf_op jit(solution)/shard_map/vmap(jit(_take))/gather | solution.py:57
  18.3 4.4 %fusion.4 = f32[32,256,128]{2,1,0:T(8,128)} fusion(bf16[32,128,256]{2,1,0:T(8,128)(2,1)} %gather_fusion.2, pred[32]{0:T(512)(128)(4,1)S(1)} %get-tuple-element.67, bf16[1,32,128,128]{3,2,1,0:T(8,128)(2,1)S(1)} %copy-done), kind=kOutput, calls=%fused_computation.12 | convolution fusion | flops 269484032 | bytes 7340064 | tf_op jit(solution)/shard_map/sgij,sgjf->sgif/dot_general | solution.py:64
  22.6 5.5 %copy.17 = f32[32,256,128]{1,0,2:T(8,128)} copy(f32[32,256,128]{2,1,0:T(8,128)} %fusion.4) | data formatting | bytes 8388608 | tf_op jit(solution)/shard_map/sgij,sgjf->sgif/dot_general | solution.py:64
  28.1 3.7 %fusion = f32[4,128,256]{2,0,1:T(4,128)S(1)} fusion(f32[32,256,128]{1,0,2:T(8,128)} %copy.17, s32[32]{0:T(128)S(1)} %subtract_bitcast_fusion, pred[32]{0:T(512)(128)(4,1)S(1)} %iota_compare_fusion.1), kind=kOutput, calls=%fused_computation.7 | convolution fusion | flops 50331904 | bytes 4718752 | tf_op jit(solution)/shard_map/sgb,sgif->sbif/dot_general | solution.py:67
  31.8 0.1 copy.16
  32.0 0.2 multiply_reduce_fusion.1
  32.2 0.1 multiply_convert_fusion.5
  32.3 0.1 dynamic-slice_bitcast_fusion
  32.4 3.2 %collective-permute-start.2 = (bf16[1,32,256]{2,1,0:T(8,128)(2,1)S(1)}, bf16[1,32,256]{2,1,0:T(8,128)(2,1)S(1)}, u32[]{:S(2)}, u32[]{:S(2)}) collective-permute-start(bf16[1,32,256]{2,1,0:T(8,128)(2,1)S(1)} %get-tuple-element.83), channel_id=1, source_target_pairs={{0,32},{32,0},{64,96},{96,64},{128,160},{160,128},{192,224},{224,1... | collective-permute-start | bytes 49160 | tf_op jit(solution)/shard_map/ppermute | solution.py:26
  35.7 4.5 %collective-permute-start.3 = (bf16[1,32,256]{2,1,0:T(8,128)(2,1)S(1)}, bf16[1,32,256]{2,1,0:T(8,128)(2,1)S(1)}, u32[]{:S(2)}, u32[]{:S(2)}) collective-permute-start(bf16[1,32,256]{2,1,0:T(8,128)(2,1)S(1)} %get-tuple-element.82), channel_id=1, source_target_pairs={{0,64},{32,96},{64,0},{96,32},{128,192},{160,224},{192,128},{224,1... | collective-permute-start | bytes 49160 | tf_op jit(solution)/shard_map/ppermute | solution.py:26
  40.2 1.9 %collective-permute-start.4 = (bf16[1,32,256]{2,1,0:T(8,128)(2,1)S(1)}, bf16[1,32,256]{2,1,0:T(8,128)(2,1)S(1)}, u32[]{:S(2)}, u32[]{:S(2)}) collective-permute-start(bf16[1,32,256]{2,1,0:T(8,128)(2,1)S(1)} %get-tuple-element.81), channel_id=1, source_target_pairs={{0,96},{32,64},{64,32},{96,0},{128,224},{160,192},{192,160},{224,1... | collective-permute-start | bytes 49160 | tf_op jit(solution)/shard_map/ppermute | solution.py:26
  42.1 3.1 %collective-permute-start.5 = (bf16[1,32,256]{2,1,0:T(8,128)(2,1)S(1)}, bf16[1,32,256]{2,1,0:T(8,128)(2,1)S(1)}, u32[]{:S(2)}, u32[]{:S(2)}) collective-permute-start(bf16[1,32,256]{2,1,0:T(8,128)(2,1)S(1)} %get-tuple-element.80), channel_id=1, source_target_pairs={{0,128},{32,160},{64,192},{96,224},{128,0},{160,32},{192,64},{224,... | collective-permute-start | bytes 49160 | tf_op jit(solution)/shard_map/ppermute | solution.py:26
  45.3 1.9 %collective-permute-start.6 = (bf16[1,32,256]{2,1,0:T(8,128)(2,1)S(1)}, bf16[1,32,256]{2,1,0:T(8,128)(2,1)S(1)}, u32[]{:S(2)}, u32[]{:S(2)}) collective-permute-start(bf16[1,32,256]{2,1,0:T(8,128)(2,1)S(1)} %get-tuple-element.79), channel_id=1, source_target_pairs={{0,160},{32,128},{64,224},{96,192},{128,32},{160,0},{192,96},{224,... | collective-permute-start | bytes 49160 | tf_op jit(solution)/shard_map/ppermute | solution.py:26
  47.2 6.6 %collective-permute-start.7 = (bf16[1,32,256]{2,1,0:T(8,128)(2,1)S(1)}, bf16[1,32,256]{2,1,0:T(8,128)(2,1)S(1)}, u32[]{:S(2)}, u32[]{:S(2)}) collective-permute-start(bf16[1,32,256]{2,1,0:T(8,128)(2,1)S(1)} %get-tuple-element.78), channel_id=1, source_target_pairs={{0,192},{32,224},{64,128},{96,160},{128,64},{160,96},{192,0},{224,... | collective-permute-start | bytes 49160 | tf_op jit(solution)/shard_map/ppermute | solution.py:26
  53.9 1.9 %collective-permute-start.8 = (bf16[1,32,256]{2,1,0:T(8,128)(2,1)S(1)}, bf16[1,32,256]{2,1,0:T(8,128)(2,1)S(1)}, u32[]{:S(2)}, u32[]{:S(2)}) collective-permute-start(bf16[1,32,256]{2,1,0:T(8,128)(2,1)S(1)} %get-tuple-element.77), channel_id=1, source_target_pairs={{0,224},{32,192},{64,160},{96,128},{128,96},{160,64},{192,32},{224... | collective-permute-start | bytes 49160 | tf_op jit(solution)/shard_map/ppermute | solution.py:26
  55.8 4.6 %collective-permute-start.9 = (bf16[1,32,256]{2,1,0:T(8,128)(2,1)S(1)}, bf16[1,32,256]{2,1,0:T(8,128)(2,1)S(1)}, u32[]{:S(2)}, u32[]{:S(2)}) collective-permute-start(bf16[1,32,256]{2,1,0:T(8,128)(2,1)S(1)} %get-tuple-element.76), channel_id=1, source_target_pairs={{0,256},{32,288},{64,320},{96,352},{128,384},{160,416},{192,448},{... | collective-permute-start | bytes 49160 | tf_op jit(solution)/shard_map/ppermute | solution.py:26
  60.5 1.9 %collective-permute-start.10 = (bf16[1,32,256]{2,1,0:T(8,128)(2,1)S(1)}, bf16[1,32,256]{2,1,0:T(8,128)(2,1)S(1)}, u32[]{:S(2)}, u32[]{:S(2)}) collective-permute-start(bf16[1,32,256]{2,1,0:T(8,128)(2,1)S(1)} %get-tuple-element.75), channel_id=1, source_target_pairs={{0,288},{32,256},{64,352},{96,320},{128,416},{160,384},{192,480},{... | collective-permute-start | bytes 49160 | tf_op jit(solution)/shard_map/ppermute | solution.py:26
  62.4 8.1 %collective-permute-start.11 = (bf16[1,32,256]{2,1,0:T(8,128)(2,1)S(1)}, bf16[1,32,256]{2,1,0:T(8,128)(2,1)S(1)}, u32[]{:S(2)}, u32[]{:S(2)}) collective-permute-start(bf16[1,32,256]{2,1,0:T(8,128)(2,1)S(1)} %get-tuple-element.74), channel_id=1, source_target_pairs={{0,320},{32,352},{64,256},{96,288},{128,448},{160,480},{192,384},{... | collective-permute-start | bytes 49160 | tf_op jit(solution)/shard_map/ppermute | solution.py:26
  70.6 1.9 %collective-permute-start.12 = (bf16[1,32,256]{2,1,0:T(8,128)(2,1)S(1)}, bf16[1,32,256]{2,1,0:T(8,128)(2,1)S(1)}, u32[]{:S(2)}, u32[]{:S(2)}) collective-permute-start(bf16[1,32,256]{2,1,0:T(8,128)(2,1)S(1)} %get-tuple-element.73), channel_id=1, source_target_pairs={{0,352},{32,320},{64,288},{96,256},{128,480},{160,448},{192,416},{... | collective-permute-start | bytes 49160 | tf_op jit(solution)/shard_map/ppermute | solution.py:26
  72.6 4.3 %collective-permute-start.13 = (bf16[1,32,256]{2,1,0:T(8,128)(2,1)S(1)}, bf16[1,32,256]{2,1,0:T(8,128)(2,1)S(1)}, u32[]{:S(2)}, u32[]{:S(2)}) collective-permute-start(bf16[1,32,256]{2,1,0:T(8,128)(2,1)S(1)} %get-tuple-element.72), channel_id=1, source_target_pairs={{0,384},{32,416},{64,448},{96,480},{128,256},{160,288},{192,320},{... | collective-permute-start | bytes 49160 | tf_op jit(solution)/shard_map/ppermute | solution.py:26
  76.9 1.9 %collective-permute-start.14 = (bf16[1,32,256]{2,1,0:T(8,128)(2,1)S(1)}, bf16[1,32,256]{2,1,0:T(8,128)(2,1)S(1)}, u32[]{:S(2)}, u32[]{:S(2)}) collective-permute-start(bf16[1,32,256]{2,1,0:T(8,128)(2,1)S(1)} %get-tuple-element.71), channel_id=1, source_target_pairs={{0,416},{32,384},{64,480},{96,448},{128,288},{160,256},{192,352},{... | collective-permute-start | bytes 49160 | tf_op jit(solution)/shard_map/ppermute | solution.py:26
  78.9 7.9 %collective-permute-start.15 = (bf16[1,32,256]{2,1,0:T(8,128)(2,1)S(1)}, bf16[1,32,256]{2,1,0:T(8,128)(2,1)S(1)}, u32[]{:S(2)}, u32[]{:S(2)}) collective-permute-start(bf16[1,32,256]{2,1,0:T(8,128)(2,1)S(1)} %get-tuple-element.70), channel_id=1, source_target_pairs={{0,448},{32,480},{64,384},{96,416},{128,320},{160,352},{192,256},{... | collective-permute-start | bytes 49160 | tf_op jit(solution)/shard_map/ppermute | solution.py:26
  86.8 1.9 %collective-permute-start.16 = (bf16[1,32,256]{2,1,0:T(8,128)(2,1)S(1)}, bf16[1,32,256]{2,1,0:T(8,128)(2,1)S(1)}, u32[]{:S(2)}, u32[]{:S(2)}) collective-permute-start(bf16[1,32,256]{2,1,0:T(8,128)(2,1)S(1)} %get-tuple-element.69), channel_id=1, source_target_pairs={{0,480},{32,448},{64,416},{96,384},{128,352},{160,320},{192,288},{... | collective-permute-start | bytes 49160 | tf_op jit(solution)/shard_map/ppermute | solution.py:26
  88.8 5.8 %collective-permute-done.16 = bf16[1,32,256]{2,1,0:T(8,128)(2,1)S(1)} collective-permute-done((bf16[1,32,256]{2,1,0:T(8,128)(2,1)S(1)}, bf16[1,32,256]{2,1,0:T(8,128)(2,1)S(1)}, u32[]{:S(2)}, u32[]{:S(2)}) %collective-permute-start.16) | collective-permute-done | bytes 16416 | tf_op jit(solution)/shard_map/ppermute | solution.py:26
  94.6 0.6 gather_fusion
  95.1 0.3 fusion.33
  95.5 0.2 slice_multiply_fusion
  95.7 0.6 while.13
  96.3 0.1 multiply_reduce_fusion
  96.5 2.7 %fusion.19 = bf16[16,32,256]{2,1,0:T(8,128)(2,1)} fusion(f32[16,32,256]{2,1,0:T(8,128)S(1)} %get-tuple-element.30, bf16[1024,256]{1,0:T(8,128)(2,1)S(1)} %copy-done.6, bf16[256,1024]{1,0:T(8,128)(2,1)} %param.27, f32[256]{0:T(256)S(1)} %copy-done.7, f32[16,32]{1,0:T(8,128)S(1)} %add_rsqrt_fusion), kind=kOutput, calls=%fused_computation.23 | convolution fusion | flops 540147712 | bytes 1838080 | tf_op jit(solution)/shard_map/tnh,hf->tnf/dot_general | solution.py:93
  99.2 3.5 %all-to-all-start = ((bf16[16,32,256]{2,1,0:T(8,128)(2,1)}), bf16[16,32,256]{2,1,0:T(8,128)(2,1)S(1)}, u32[]{:S(2)}, u32[]{:S(2)}) async-start(bf16[16,32,256]{2,1,0:T(8,128)(2,1)} %fusion.19), calls=%async_computation | async-start | bytes 524288 | tf_op jit(solution)/shard_map/all_to_all | solution.py:134
  102.8 7.3 %all-to-all-done = bf16[16,32,256]{2,1,0:T(8,128)(2,1)S(1)} async-done(((bf16[16,32,256]{2,1,0:T(8,128)(2,1)}), bf16[16,32,256]{2,1,0:T(8,128)(2,1)S(1)}, u32[]{:S(2)}, u32[]{:S(2)}) %all-to-all-start) | async-done | bytes 262176 | tf_op jit(solution)/shard_map/all_to_all | solution.py:134
  110.1 8.0 %collective-permute-start.17 = (bf16[1,512,256]{2,1,0:T(8,128)(2,1)S(1)}, bf16[1,512,256]{2,1,0:T(8,128)(2,1)S(1)}, u32[]{:S(2)}, u32[]{:S(2)}) collective-permute-start(bf16[1,512,256]{2,1,0:T(8,128)(2,1)S(1)} %bitcast.167), channel_id=1, source_target_pairs={{0,1},{1,2},{2,3},{3,4},{4,5},{5,6},{6,7},{7,8},{8,9},{9,10},{10,1... | collective-permute-start | bytes 786440 | tf_op jit(solution)/shard_map/ppermute | solution.py:39
  118.1 1.9 %collective-permute-start.18 = (bf16[1,512,256]{2,1,0:T(8,128)(2,1)S(1)}, bf16[1,512,256]{2,1,0:T(8,128)(2,1)S(1)}, u32[]{:S(2)}, u32[]{:S(2)}) collective-permute-start(bf16[1,512,256]{2,1,0:T(8,128)(2,1)S(1)} %bitcast.168), channel_id=1, source_target_pairs={{1,0},{2,1},{3,2},{4,3},{5,4},{6,5},{7,6},{8,7},{9,8},{10,9},{11,1... | collective-permute-start | bytes 786440 | tf_op jit(solution)/shard_map/ppermute | solution.py:41
  120.0 0.2 convolution_convert_fusion
  120.3 2.0 %gather_fusion.1 = bf16[32,128,256]{2,1,0:T(8,128)(2,1)} fusion(bf16[1,4,128,256]{3,2,1,0:T(8,128)(2,1)S(1)} %bitcast.162, s32[32]{0:T(128)S(1)} %or_bitcast_fusion.2), kind=kCustom, calls=%fused_computation.3 | custom fusion | bytes 4194560 | tf_op jit(solution)/shard_map/vmap(jit(_take))/gather | solution.py:57
  122.3 4.7 %collective-permute-done.18 = bf16[1,512,256]{2,1,0:T(8,128)(2,1)S(1)} collective-permute-done((bf16[1,512,256]{2,1,0:T(8,128)(2,1)S(1)}, bf16[1,512,256]{2,1,0:T(8,128)(2,1)S(1)}, u32[]{:S(2)}, u32[]{:S(2)}) %collective-permute-start.18) | collective-permute-done | bytes 262176 | tf_op jit(solution)/shard_map/ppermute | solution.py:41
  127.0 0.1 pad_maximum_fusion.1
  127.1 2.0 %gather_fusion.3 = bf16[32,128,256]{2,1,0:T(8,128)(2,1)} fusion(bf16[1,12,128,256]{3,2,1,0:T(8,128)(2,1)S(1)} %bitcast.164, s32[32]{0:T(128)S(1)} %or_bitcast_fusion), kind=kCustom, calls=%fused_computation.1.clone | custom fusion | bytes 4194560 | tf_op jit(solution)/shard_map/vmap(jit(_take))/gather | solution.py:57
  129.1 4.0 %fusion.14 = bf16[1,32,128,128]{3,2,1,0:T(8,128)(2,1)} fusion(bf16[32,128,256]{2,1,0:T(8,128)(2,1)} %gather_fusion.3, pred[32]{0:T(512)(128)(4,1)S(1)} %get-tuple-element.63, bf16[32,128,256]{2,1,0:T(8,128)(2,1)} %gather_fusion.1, pred[32]{0:T(512)(128)(4,1)S(1)} %get-tuple-element.85), kind=kOutput, calls=%fused_computation.21 | convolution fusion | flops 271581184 | bytes 5242944 | tf_op jit(solution)/shard_map/spif,spjf->spij/dot_general | solution.py:146
  133.1 0.7 copy.45
  (77 shorter events, 0.5 us)
Async XLA Ops:
  0.6 17.6 %copy-start = (bf16[1,32,128,128]{3,2,1,0:T(8,128)(2,1)S(1)}, bf16[1,32,128,128]{3,2,1,0:T(8,128)(2,1)}, u32[]{:S(2)}) copy-start(bf16[1,32,128,128]{3,2,1,0:T(8,128)(2,1)} %param.22) | copy-start | bytes 3145732
  0.6 10.1 %collective-permute-start = (bf16[1,512,256]{2,1,0:T(8,128)(2,1)}, bf16[1,512,256]{2,1,0:T(8,128)(2,1)S(1)}, u32[]{:S(2)}, u32[]{:S(2)}) collective-permute-start(bf16[1,512,256]{2,1,0:T(8,128)(2,1)} %param.18), channel_id=1, source_target_pairs={{0,1},{1,2},{2,3},{3,4},{4,5},{5,6},{6,7},{7,8},{8,9},{9,10},{10,1... | collective-permute-start | bytes 786440 | tf_op jit(solution)/shard_map/ppermute | solution.py:39
  6.1 9.1 %collective-permute-start.1 = (bf16[1,512,256]{2,1,0:T(8,128)(2,1)}, bf16[1,512,256]{2,1,0:T(8,128)(2,1)S(1)}, u32[]{:S(2)}, u32[]{:S(2)}) collective-permute-start(bf16[1,512,256]{2,1,0:T(8,128)(2,1)} %param.18), channel_id=1, source_target_pairs={{1,0},{2,1},{3,2},{4,3},{5,4},{6,5},{7,6},{8,7},{9,8},{10,9},{11,1... | collective-permute-start | bytes 786440 | tf_op jit(solution)/shard_map/ppermute | solution.py:41
  28.1 3.8 %copy-start.1 = (bf16[1,512,256]{2,1,0:T(8,128)(2,1)S(1)}, bf16[1,512,256]{2,1,0:T(8,128)(2,1)}, u32[]{:S(2)}) copy-start(bf16[1,512,256]{2,1,0:T(8,128)(2,1)} %param.18) | copy-start | bytes 786436
  28.1 4.0 %copy-start.5 = (f32[256]{0:T(256)S(1)}, f32[256]{0:T(256)}, u32[]{:S(2)}) copy-start(f32[256]{0:T(256)} %param.23) | copy-start | bytes 3076
  31.8 3.8 %copy-start.4 = (f32[16,256]{1,0:T(8,128)S(1)}, f32[16,256]{1,0:T(8,128)}, u32[]{:S(2)}) copy-start(f32[16,256]{1,0:T(8,128)} %param.25) | copy-start | bytes 49156
  31.8 63.3 %copy-start.2 = (bf16[256,512]{1,0:T(8,128)(2,1)S(1)}, bf16[256,512]{1,0:T(8,128)(2,1)}, u32[]{:S(2)}) copy-start(bf16[256,512]{1,0:T(8,128)(2,1)} %param.24) | copy-start | bytes 786436
  32.4 14.8 %collective-permute-start.2 = (bf16[1,32,256]{2,1,0:T(8,128)(2,1)S(1)}, bf16[1,32,256]{2,1,0:T(8,128)(2,1)S(1)}, u32[]{:S(2)}, u32[]{:S(2)}) collective-permute-start(bf16[1,32,256]{2,1,0:T(8,128)(2,1)S(1)} %get-tuple-element.83), channel_id=1, source_target_pairs={{0,32},{32,0},{64,96},{96,64},{128,160},{160,128},{192,224},{224,1... | collective-permute-start | bytes 49160 | tf_op jit(solution)/shard_map/ppermute | solution.py:26
  35.7 18.2 %collective-permute-start.3 = (bf16[1,32,256]{2,1,0:T(8,128)(2,1)S(1)}, bf16[1,32,256]{2,1,0:T(8,128)(2,1)S(1)}, u32[]{:S(2)}, u32[]{:S(2)}) collective-permute-start(bf16[1,32,256]{2,1,0:T(8,128)(2,1)S(1)} %get-tuple-element.82), channel_id=1, source_target_pairs={{0,64},{32,96},{64,0},{96,32},{128,192},{160,224},{192,128},{224,1... | collective-permute-start | bytes 49160 | tf_op jit(solution)/shard_map/ppermute | solution.py:26
  40.2 15.6 %collective-permute-start.4 = (bf16[1,32,256]{2,1,0:T(8,128)(2,1)S(1)}, bf16[1,32,256]{2,1,0:T(8,128)(2,1)S(1)}, u32[]{:S(2)}, u32[]{:S(2)}) collective-permute-start(bf16[1,32,256]{2,1,0:T(8,128)(2,1)S(1)} %get-tuple-element.81), channel_id=1, source_target_pairs={{0,96},{32,64},{64,32},{96,0},{128,224},{160,192},{192,160},{224,1... | collective-permute-start | bytes 49160 | tf_op jit(solution)/shard_map/ppermute | solution.py:26
  42.1 18.3 %collective-permute-start.5 = (bf16[1,32,256]{2,1,0:T(8,128)(2,1)S(1)}, bf16[1,32,256]{2,1,0:T(8,128)(2,1)S(1)}, u32[]{:S(2)}, u32[]{:S(2)}) collective-permute-start(bf16[1,32,256]{2,1,0:T(8,128)(2,1)S(1)} %get-tuple-element.80), channel_id=1, source_target_pairs={{0,128},{32,160},{64,192},{96,224},{128,0},{160,32},{192,64},{224,... | collective-permute-start | bytes 49160 | tf_op jit(solution)/shard_map/ppermute | solution.py:26
  45.3 17.2 %collective-permute-start.6 = (bf16[1,32,256]{2,1,0:T(8,128)(2,1)S(1)}, bf16[1,32,256]{2,1,0:T(8,128)(2,1)S(1)}, u32[]{:S(2)}, u32[]{:S(2)}) collective-permute-start(bf16[1,32,256]{2,1,0:T(8,128)(2,1)S(1)} %get-tuple-element.79), channel_id=1, source_target_pairs={{0,160},{32,128},{64,224},{96,192},{128,32},{160,0},{192,96},{224,... | collective-permute-start | bytes 49160 | tf_op jit(solution)/shard_map/ppermute | solution.py:26
  47.2 23.4 %collective-permute-start.7 = (bf16[1,32,256]{2,1,0:T(8,128)(2,1)S(1)}, bf16[1,32,256]{2,1,0:T(8,128)(2,1)S(1)}, u32[]{:S(2)}, u32[]{:S(2)}) collective-permute-start(bf16[1,32,256]{2,1,0:T(8,128)(2,1)S(1)} %get-tuple-element.78), channel_id=1, source_target_pairs={{0,192},{32,224},{64,128},{96,160},{128,64},{160,96},{192,0},{224,... | collective-permute-start | bytes 49160 | tf_op jit(solution)/shard_map/ppermute | solution.py:26
  53.9 18.7 %collective-permute-start.8 = (bf16[1,32,256]{2,1,0:T(8,128)(2,1)S(1)}, bf16[1,32,256]{2,1,0:T(8,128)(2,1)S(1)}, u32[]{:S(2)}, u32[]{:S(2)}) collective-permute-start(bf16[1,32,256]{2,1,0:T(8,128)(2,1)S(1)} %get-tuple-element.77), channel_id=1, source_target_pairs={{0,224},{32,192},{64,160},{96,128},{128,96},{160,64},{192,32},{224... | collective-permute-start | bytes 49160 | tf_op jit(solution)/shard_map/ppermute | solution.py:26
  55.8 21.1 %collective-permute-start.9 = (bf16[1,32,256]{2,1,0:T(8,128)(2,1)S(1)}, bf16[1,32,256]{2,1,0:T(8,128)(2,1)S(1)}, u32[]{:S(2)}, u32[]{:S(2)}) collective-permute-start(bf16[1,32,256]{2,1,0:T(8,128)(2,1)S(1)} %get-tuple-element.76), channel_id=1, source_target_pairs={{0,256},{32,288},{64,320},{96,352},{128,384},{160,416},{192,448},{... | collective-permute-start | bytes 49160 | tf_op jit(solution)/shard_map/ppermute | solution.py:26
  60.5 18.4 %collective-permute-start.10 = (bf16[1,32,256]{2,1,0:T(8,128)(2,1)S(1)}, bf16[1,32,256]{2,1,0:T(8,128)(2,1)S(1)}, u32[]{:S(2)}, u32[]{:S(2)}) collective-permute-start(bf16[1,32,256]{2,1,0:T(8,128)(2,1)S(1)} %get-tuple-element.75), channel_id=1, source_target_pairs={{0,288},{32,256},{64,352},{96,320},{128,416},{160,384},{192,480},{... | collective-permute-start | bytes 49160 | tf_op jit(solution)/shard_map/ppermute | solution.py:26
  62.4 24.3 %collective-permute-start.11 = (bf16[1,32,256]{2,1,0:T(8,128)(2,1)S(1)}, bf16[1,32,256]{2,1,0:T(8,128)(2,1)S(1)}, u32[]{:S(2)}, u32[]{:S(2)}) collective-permute-start(bf16[1,32,256]{2,1,0:T(8,128)(2,1)S(1)} %get-tuple-element.74), channel_id=1, source_target_pairs={{0,320},{32,352},{64,256},{96,288},{128,448},{160,480},{192,384},{... | collective-permute-start | bytes 49160 | tf_op jit(solution)/shard_map/ppermute | solution.py:26
  70.6 18.1 %collective-permute-start.12 = (bf16[1,32,256]{2,1,0:T(8,128)(2,1)S(1)}, bf16[1,32,256]{2,1,0:T(8,128)(2,1)S(1)}, u32[]{:S(2)}, u32[]{:S(2)}) collective-permute-start(bf16[1,32,256]{2,1,0:T(8,128)(2,1)S(1)} %get-tuple-element.73), channel_id=1, source_target_pairs={{0,352},{32,320},{64,288},{96,256},{128,480},{160,448},{192,416},{... | collective-permute-start | bytes 49160 | tf_op jit(solution)/shard_map/ppermute | solution.py:26
  72.6 16.2 %collective-permute-start.13 = (bf16[1,32,256]{2,1,0:T(8,128)(2,1)S(1)}, bf16[1,32,256]{2,1,0:T(8,128)(2,1)S(1)}, u32[]{:S(2)}, u32[]{:S(2)}) collective-permute-start(bf16[1,32,256]{2,1,0:T(8,128)(2,1)S(1)} %get-tuple-element.72), channel_id=1, source_target_pairs={{0,384},{32,416},{64,448},{96,480},{128,256},{160,288},{192,320},{... | collective-permute-start | bytes 49160 | tf_op jit(solution)/shard_map/ppermute | solution.py:26
  76.9 11.8 %collective-permute-start.14 = (bf16[1,32,256]{2,1,0:T(8,128)(2,1)S(1)}, bf16[1,32,256]{2,1,0:T(8,128)(2,1)S(1)}, u32[]{:S(2)}, u32[]{:S(2)}) collective-permute-start(bf16[1,32,256]{2,1,0:T(8,128)(2,1)S(1)} %get-tuple-element.71), channel_id=1, source_target_pairs={{0,416},{32,384},{64,480},{96,448},{128,288},{160,256},{192,352},{... | collective-permute-start | bytes 49160 | tf_op jit(solution)/shard_map/ppermute | solution.py:26
  78.9 9.9 %collective-permute-start.15 = (bf16[1,32,256]{2,1,0:T(8,128)(2,1)S(1)}, bf16[1,32,256]{2,1,0:T(8,128)(2,1)S(1)}, u32[]{:S(2)}, u32[]{:S(2)}) collective-permute-start(bf16[1,32,256]{2,1,0:T(8,128)(2,1)S(1)} %get-tuple-element.70), channel_id=1, source_target_pairs={{0,448},{32,480},{64,384},{96,416},{128,320},{160,352},{192,256},{... | collective-permute-start | bytes 49160 | tf_op jit(solution)/shard_map/ppermute | solution.py:26
  86.8 7.8 %collective-permute-start.16 = (bf16[1,32,256]{2,1,0:T(8,128)(2,1)S(1)}, bf16[1,32,256]{2,1,0:T(8,128)(2,1)S(1)}, u32[]{:S(2)}, u32[]{:S(2)}) collective-permute-start(bf16[1,32,256]{2,1,0:T(8,128)(2,1)S(1)} %get-tuple-element.69), channel_id=1, source_target_pairs={{0,480},{32,448},{64,416},{96,384},{128,352},{160,320},{192,288},{... | collective-permute-start | bytes 49160 | tf_op jit(solution)/shard_map/ppermute | solution.py:26
  95.4 1.1 copy-start.6
  95.4 1.1 copy-start.7
  96.5 23.5 %copy-start.3 = (bf16[256,256]{1,0:T(8,128)(2,1)S(1)}, bf16[256,256]{1,0:T(8,128)(2,1)}, u32[]{:S(2)}) copy-start(bf16[256,256]{1,0:T(8,128)(2,1)} %param.29) | copy-start | bytes 393220
  99.2 10.9 %all-to-all-start = ((bf16[16,32,256]{2,1,0:T(8,128)(2,1)}), bf16[16,32,256]{2,1,0:T(8,128)(2,1)S(1)}, u32[]{:S(2)}, u32[]{:S(2)}) async-start(bf16[16,32,256]{2,1,0:T(8,128)(2,1)} %fusion.19), calls=%async_computation | async-start | bytes 524288 | tf_op jit(solution)/shard_map/all_to_all | solution.py:134
  110.1 12.2 %collective-permute-start.17 = (bf16[1,512,256]{2,1,0:T(8,128)(2,1)S(1)}, bf16[1,512,256]{2,1,0:T(8,128)(2,1)S(1)}, u32[]{:S(2)}, u32[]{:S(2)}) collective-permute-start(bf16[1,512,256]{2,1,0:T(8,128)(2,1)S(1)} %bitcast.167), channel_id=1, source_target_pairs={{0,1},{1,2},{2,3},{3,4},{4,5},{5,6},{6,7},{7,8},{8,9},{9,10},{10,1... | collective-permute-start | bytes 786440 | tf_op jit(solution)/shard_map/ppermute | solution.py:39
  118.1 8.9 %collective-permute-start.18 = (bf16[1,512,256]{2,1,0:T(8,128)(2,1)S(1)}, bf16[1,512,256]{2,1,0:T(8,128)(2,1)S(1)}, u32[]{:S(2)}, u32[]{:S(2)}) collective-permute-start(bf16[1,512,256]{2,1,0:T(8,128)(2,1)S(1)} %bitcast.168), channel_id=1, source_target_pairs={{1,0},{2,1},{3,2},{4,3},{5,4},{6,5},{7,6},{8,7},{9,8},{10,9},{11,1... | collective-permute-start | bytes 786440 | tf_op jit(solution)/shard_map/ppermute | solution.py:41
